TPU v7x, 128 devices: a whole 4x4x4 slice. The times are simulated.
128 devices in a mesh: queue: 16 (over y_hi, z, core), head: 8 (over y_lo, x).
Axes of the slice: x: 4, y: 4 (y_hi: 2, y_lo: 2; y = y_hi * 2 + y_lo), z: 4, core: 2. Of those that a mesh axis runs over, the one named last changes fastest.
Arguments:
- latent: bfloat16 [4096, 5120], P(('queue', 'head')), may hold values from -6 to 6
- fresh: bfloat16 [256, 5120], P('head'), may hold values from -6 to 6
- levels: int32 [16], replicated, may hold values from 0 to 47, as said below
- windows: int32 [16], replicated, may hold values from 1 to 16, as said below
- plan: int32 [48], replicated, may hold values from 20 to 975, as said below
- mod_table: float32 [3, 5120], replicated, may hold values from -3 to 3
- w_query: bfloat16 [5120, 4096], P(None, 'head'), may hold values from -0.078125 to 0.078125
- w_key: bfloat16 [5120, 4096], P(None, 'head'), may hold values from -0.078125 to 0.078125
- w_value: bfloat16 [5120, 4096], P(None, 'head'), may hold values from -0.078125 to 0.078125
- w_out: bfloat16 [4096, 5120], P('head'), may hold values from -0.09375 to 0.09375
- query_gain: float32 [4096], P('head'), may hold values from 0.7 to 4, as said below
- key_gain: float32 [4096], P('head'), may hold values from 0.7 to 4, as said below
Outputs:
- velocity: bfloat16 [2, 4096, 5120], P(None, ('queue', 'head'))
- updated: bfloat16 [4096, 5120], P(('queue', 'head'))
Inputs may be any that keep to these rules, and one draw needn't show every extreme that they name: `levels`: strictly rising from slot to slot; the first slot has level 0 and the last level 47. `windows`: some slot has window 16 and some slot window 1. `plan`: strictly rising. `query_gain`: positive. `key_gain`: positive.
All inputs are finite; a program needn't handle non-finite values.
Results may differ from a plain program's by a relative error of at most 0.035.
Values may be sent and summed in bfloat16 or wider, within the bound.
No kernel may reach another device: no remote copies, remote signals or barrier semaphores. Data moves between devices by JAX's collectives and lax.ppermute only.
A program may use at most 128 MiB of HBM per device.

v0:
```python
import math

import jax
import jax.numpy as jnp
from jax import lax
from jax.sharding import PartitionSpec as P

HD = 128
STEPS = 2


def shifted(array, axis, by):
    length = lax.axis_size(axis)
    pairs = [(i, i + by) for i in range(length) if 0 <= i + by < length]
    return lax.ppermute(array, axis, pairs)


def embed(times, width):
    half = width // 2
    freq = jnp.exp(-math.log(10000.0) * jnp.arange(half, dtype=jnp.float32) / half)
    angle = times[:, None] * freq[None, :]
    return jnp.concatenate([jnp.cos(angle), jnp.sin(angle)], axis=-1)


def absorb(carry, keys, values, first_row, queries, lower, slot, span):
    top, total, summed = carry
    count = keys.shape[0]
    heads_local = keys.shape[1] // HD
    key_heads = keys.reshape(count, heads_local, HD)
    value_heads = values.reshape(count, heads_local, HD)
    scores = jnp.einsum(
        "qhd,khd->hqk", queries, key_heads, preferred_element_type=jnp.float32
    ) / math.sqrt(HD)
    span_ids = (first_row + jnp.arange(count, dtype=jnp.int32)) // span
    valid = ((span_ids >= lower) & (span_ids <= slot))[None, None, :]
    masked = jnp.where(valid, scores, -1e30)
    new_top = jnp.maximum(top, jnp.max(masked, axis=-1))
    weights = jnp.where(valid, jnp.exp(scores - new_top[:, :, None]), 0.0)
    fade = jnp.exp(top - new_top)
    total = total * fade + jnp.sum(weights, axis=-1)
    summed = summed * fade[:, :, None] + jnp.einsum(
        "hqk,khd->hqd",
        weights.astype(jnp.bfloat16),
        value_heads,
        preferred_element_type=jnp.float32,
    )
    return (new_top, total, summed)


def on_device(
    latent,
    fresh,
    levels,
    windows,
    plan,
    mod_table,
    w_query,
    w_key,
    w_value,
    w_out,
    query_gain,
    key_gain,
):
    queue_count = lax.axis_size("queue")
    head_count = lax.axis_size("head")
    slot = lax.axis_index("queue")
    rows = latent.shape[0]
    span = rows * head_count
    features = w_query.shape[1]
    heads_local = features // HD
    table_hits = levels[:, None] == jnp.arange(plan.shape[0], dtype=jnp.int32)[None, :]
    t_all = jnp.sum(jnp.where(table_hits, plan[None, :], 0), axis=1).astype(jnp.float32)
    t_from = t_all[slot]
    t_to = jnp.where(slot > 0, t_all[jnp.maximum(slot - 1, 0)], 0.0)
    step_size = (t_to - t_from) / 1000.0
    lower = jnp.maximum(0, slot - windows[slot] + 1)
    emb = embed(t_from[None], latent.shape[1])[0]
    shift = mod_table[0] + emb
    scale = mod_table[1] + emb
    gate = mod_table[2] + emb
    state = latent
    speeds = []
    new = latent
    for step in range(STEPS):
        x = state.astype(jnp.float32)
        mean = jnp.mean(x, axis=-1, keepdims=True)
        var = jnp.mean((x - mean) ** 2, axis=-1, keepdims=True)
        normed = ((x - mean) * lax.rsqrt(var + 1e-06) * (1.0 + scale) + shift).astype(jnp.bfloat16)
        piece = lax.all_gather(normed, "head", axis=0, tiled=True)
        projected = jnp.concatenate(
            [
                jnp.dot(piece, w_query, preferred_element_type=jnp.float32),
                jnp.dot(piece, w_key, preferred_element_type=jnp.float32),
                jnp.dot(piece, w_value, preferred_element_type=jnp.float32),
            ],
            axis=-1,
        )
        q = projected[:, :features]
        k = projected[:, features : 2 * features]
        values = projected[:, 2 * features :].astype(jnp.bfloat16)
        query_sq, key_sq = lax.psum((jnp.sum(q * q, axis=-1), jnp.sum(k * k, axis=-1)), "head")
        every = features * head_count
        queries = (q * lax.rsqrt(query_sq / every + 1e-06)[:, None] * query_gain).astype(
            jnp.bfloat16
        )
        keys = (k * lax.rsqrt(key_sq / every + 1e-06)[:, None] * key_gain).astype(jnp.bfloat16)
        query_heads = queries.reshape(span, heads_local, HD)
        start_carry = (
            jnp.full((heads_local, span), -1e30, jnp.float32),
            jnp.zeros((heads_local, span), jnp.float32),
            jnp.zeros((heads_local, span, HD), jnp.float32),
        )
        inner = start_carry
        piece_keys = lax.all_gather(keys, "queue", axis=0, tiled=True)
        piece_values = lax.all_gather(values, "queue", axis=0, tiled=True)
        count = piece_keys.shape[0]
        blocks = count // span

        def one_block(running, block):
            block_keys, block_values, block_index = block
            return (
                absorb(
                    running,
                    block_keys,
                    block_values,
                    block_index * span,
                    query_heads,
                    lower,
                    slot,
                    span,
                ),
                None,
            )

        inner, unused = lax.scan(
            one_block,
            inner,
            (
                piece_keys.reshape(blocks, span, features),
                piece_values.reshape(blocks, span, features),
                jnp.arange(blocks, dtype=jnp.int32),
            ),
        )
        top, total, summed = inner
        attn = (
            jnp.transpose(summed / total[:, :, None], (1, 0, 2))
            .reshape(span, features)
            .astype(jnp.bfloat16)
        )
        mixed = lax.psum_scatter(
            jnp.dot(attn, w_out, preferred_element_type=jnp.float32).astype(jnp.bfloat16),
            "head",
            scatter_dimension=0,
            tiled=True,
        ).astype(jnp.float32)
        speed = (x + gate * mixed).astype(jnp.bfloat16)
        speeds.append(speed)
        new = (x + step_size * speed.astype(jnp.float32)).astype(jnp.bfloat16)
        if step < STEPS - 1:
            moved = shifted(new, "queue", -1)
            state = jnp.where(slot == queue_count - 1, fresh, moved)
    return (jnp.stack(speeds), new)


def solution(mesh):
    return jax.shard_map(
        on_device,
        mesh=mesh,
        in_specs=(
            P(("queue", "head"), None),
            P("head", None),
            P(),
            P(),
            P(),
            P(),
            P(None, "head"),
            P(None, "head"),
            P(None, "head"),
            P("head", None),
            P("head"),
            P("head"),
        ),
        out_specs=(P(None, ("queue", "head"), None), P(("queue", "head"), None)),
        check_vma=False,
    )
```

profile of v0, /device:TPU:0, one launch (start us, length us, event | category | flops | bytes accessed | tf_op | source)
XLA Modules:
  0.0 574.6 jit_solution(14695138963098198644)
XLA Ops:
  8.1 1.1 convert_reduce_fusion.1
  9.2 1.2 fusion.18
  12.0 1.1 slice_add_fusion.1
  13.1 1.9 fusion.21
  15.1 44.5 %all-gather.7.cloned.1.call-done = bf16[256,5120]{1,0:T(8,128)(2,1)} async-done(((bf16[32,5120]{1,0:T(8,128)(2,1)}), bf16[256,5120]{1,0:T(8,128)(2,1)}) %all-gather.7.cloned.1.call-update) | async-done | bytes 2621456 | tf_op jit(solution)/shard_map/all_gather | solution.py:89
  59.6 5.5 convolution_convert_fusion.3
  65.2 5.0 multiply_reduce_fusion.2
  70.3 4.1 multiply_reduce_fusion.3
  74.4 18.2 %all-reduce.1 = (f32[256]{0:T(256)S(1)}, f32[256]{0:T(256)S(1)}) all-reduce(f32[256]{0:T(256)S(1)} %get-tuple-element.453, f32[256]{0:T(256)S(1)} %get-tuple-element.455), channel_id=1, replica_groups=mesh['queue'=16,'head'=8] {'head'}, use_global_device_ids=true, to_apply=%region_4.5 | all-reduce | flops 512 | bytes 4096 | tf_op jit(solution)/shard_map/psum | solution.py:101
  94.9 25.7 %all-gather.11.cloned.1.call-done = bf16[4096,512]{1,0:T(8,128)(2,1)} async-done(((bf16[256,512]{1,0:T(8,128)(2,1)}), bf16[4096,512]{1,0:T(8,128)(2,1)}) %all-gather.11.cloned.1.call-update) | async-done | bytes 4194320 | tf_op jit(solution)/shard_map/all_gather | solution.py:115
  120.6 56.2 %all-gather.9.cloned.1.call-done = bf16[4096,512]{1,0:T(8,128)(2,1)} async-done(((bf16[256,512]{1,0:T(8,128)(2,1)}), bf16[4096,512]{1,0:T(8,128)(2,1)}) %all-gather.9.cloned.1.call-update) | async-done | bytes 4194320 | tf_op jit(solution)/shard_map/all_gather | solution.py:114
  176.8 61.6 %while.34 = (s32[]{:T(128)}, f32[4,256]{1,0:T(4,128)S(1)}, f32[4,256]{1,0:T(4,128)S(1)}, f32[4,256,128]{2,1,0:T(8,128)S(1)}, s32[16]{0:T(128)S(1)}, /*index=5*/s...) while((s32[]{:T(128)}, f32[4,256]{1,0:T(4,128)S(1)}, ...), condition=%wide.region_10.11_spmd.clone, body=%wide.region_7.10_spmd.clone.sunk | while | flops 136980224 | bytes 7144633 | solution.py:135
  178.1 1.1 constant_dynamic-slice_fusion.6
  182.0 1.1 constant_dynamic-slice_fusion.6
  189.6 1.1 constant_dynamic-slice_fusion.6
  201.2 1.1 constant_dynamic-slice_fusion.6
  238.7 5.6 convolution_convert_fusion.1
  245.6 41.1 %reduce-scatter.3.cloned.1.call-done = bf16[32,5120]{1,0:T(8,128)(2,1)} async-done(((bf16[256,5120]{1,0:T(8,128)(2,1)}), bf16[32,5120]{1,0:T(8,128)(2,1)}) %reduce-scatter.3.cloned.1.call-update) | async-done | bytes 327696 | tf_op jit(solution)/shard_map/reduce_scatter | solution.py:150
  286.7 1.1 fusion.29
  287.8 1.3 collective-permute-start
  289.1 2.2 collective-permute-done
  292.9 45.0 %all-gather.13.cloned.1.call-done = bf16[256,5120]{1,0:T(8,128)(2,1)} async-done(((bf16[32,5120]{1,0:T(8,128)(2,1)}), bf16[256,5120]{1,0:T(8,128)(2,1)}) %all-gather.13.cloned.1.call-update) | async-done | bytes 2621456 | tf_op jit(solution)/shard_map/all_gather | solution.py:89
  337.9 5.5 convolution_convert_fusion.2
  343.5 5.0 multiply_reduce_fusion
  348.5 4.1 multiply_reduce_fusion.1
  352.6 18.2 %all-reduce = (f32[256]{0:T(256)S(1)}, f32[256]{0:T(256)S(1)}) all-reduce(f32[256]{0:T(256)S(1)} %get-tuple-element.457, f32[256]{0:T(256)S(1)} %get-tuple-element.459), channel_id=1, replica_groups=mesh['queue'=16,'head'=8] {'head'}, use_global_device_ids=true, to_apply=%region_15.16 | all-reduce | flops 512 | bytes 4096 | tf_op jit(solution)/shard_map/psum | solution.py:101
  372.1 26.8 %all-gather.17.cloned.1.call-done = bf16[4096,512]{1,0:T(8,128)(2,1)} async-done(((bf16[256,512]{1,0:T(8,128)(2,1)}), bf16[4096,512]{1,0:T(8,128)(2,1)}) %all-gather.17.cloned.1.call-update) | async-done | bytes 4194320 | tf_op jit(solution)/shard_map/all_gather | solution.py:115
  398.9 56.2 %all-gather.15.cloned.1.call-done = bf16[4096,512]{1,0:T(8,128)(2,1)} async-done(((bf16[256,512]{1,0:T(8,128)(2,1)}), bf16[4096,512]{1,0:T(8,128)(2,1)}) %all-gather.15.cloned.1.call-update) | async-done | bytes 4194320 | tf_op jit(solution)/shard_map/all_gather | solution.py:114
  455.1 61.7 %while.35 = (s32[]{:T(128)}, f32[4,256]{1,0:T(4,128)S(1)}, f32[4,256]{1,0:T(4,128)S(1)}, f32[4,256,128]{2,1,0:T(8,128)S(1)}, s32[16]{0:T(128)S(1)}, /*index=5*/s...) while((s32[]{:T(128)}, f32[4,256]{1,0:T(4,128)S(1)}, ...), condition=%wide.region_21.22_spmd.clone, body=%wide.region_18.21_spmd.clone.sunk | while | flops 136980224 | bytes 7144633 | solution.py:135
  517.1 5.6 convolution_convert_fusion
  522.7 42.4 %reduce-scatter.5.cloned.1.call-done = bf16[32,5120]{1,0:T(8,128)(2,1)} async-done(((bf16[256,5120]{1,0:T(8,128)(2,1)}), bf16[32,5120]{1,0:T(8,128)(2,1)}) %reduce-scatter.5.cloned.1.call-update) | async-done | bytes 327696 | tf_op jit(solution)/shard_map/reduce_scatter | solution.py:150
  565.1 1.9 fusion.25
  (411 shorter events, 104.5 us)
Async XLA Ops:
  7.2 52.4 %all-gather.7.cloned.1.call-start = ((), (), s32[]{:S(2)}) async-start(), calls=%async_computation.2 | async-start | bytes 2949120 | tf_op jit(solution)/shard_map/all_gather | solution.py:89
  15.0 105.6 %all-gather.11.cloned.1.call-start = ((), (), s32[]{:S(2)}) async-start(), calls=%async_computation.4 | async-start | bytes 4456448 | tf_op jit(solution)/shard_map/all_gather | solution.py:115
  65.1 111.7 %all-gather.9.cloned.1.call-start = ((), (), s32[]{:S(2)}) async-start(), calls=%async_computation.3 | async-start | bytes 4456448 | tf_op jit(solution)/shard_map/all_gather | solution.py:114
  65.2 5.0 copy-start.4
  70.2 22.4 %copy-start.2 = (f32[512]{0:T(512)S(1)}, f32[512]{0:T(512)}, u32[]{:S(2)}) copy-start(f32[512]{0:T(512)} %param.27) | copy-start | bytes 6148
  70.2 23.3 %copy-start.6 = (s32[16]{0:T(128)S(1)}, s32[16]{0:T(128)}, u32[]{:S(2)}) copy-start(s32[16]{0:T(128)} %param.19) | copy-start | bytes 196
  70.2 24.5 %copy-start.3 = (f32[512]{0:T(512)S(1)}, f32[512]{0:T(512)}, u32[]{:S(2)}) copy-start(f32[512]{0:T(512)} %param.26) | copy-start | bytes 6148
  93.4 193.3 %reduce-scatter.3.cloned.1.call-start = ((), (), s32[]{:S(2)}) async-start(), calls=%async_computation.5 | async-start | bytes 2949120 | tf_op jit(solution)/shard_map/reduce_scatter | solution.py:150
  238.7 48.0 %copy-start = (bf16[32,5120]{1,0:T(8,128)(2,1)S(1)}, bf16[32,5120]{1,0:T(8,128)(2,1)}, u32[]{:S(2)}) copy-start(bf16[32,5120]{1,0:T(8,128)(2,1)} %param.16) | copy-start | bytes 983044
  244.3 47.1 %copy-start.1 = (bf16[32,5120]{1,0:T(8,128)(2,1)S(1)}, bf16[32,5120]{1,0:T(8,128)(2,1)}, u32[]{:S(2)}) copy-start(bf16[32,5120]{1,0:T(8,128)(2,1)} %param.17) | copy-start | bytes 983044
  244.3 93.6 %all-gather.13.cloned.1.call-start = ((), (), s32[]{:S(2)}) async-start(), calls=%async_computation.6 | async-start | bytes 2949120 | tf_op jit(solution)/shard_map/all_gather | solution.py:89
  287.8 3.5 collective-permute-start
  292.8 106.1 %all-gather.17.cloned.1.call-start = ((), (), s32[]{:S(2)}) async-start(), calls=%async_computation.8 | async-start | bytes 4456448 | tf_op jit(solution)/shard_map/all_gather | solution.py:115
  343.4 111.7 %all-gather.15.cloned.1.call-start = ((), (), s32[]{:S(2)}) async-start(), calls=%async_computation.7 | async-start | bytes 4456448 | tf_op jit(solution)/shard_map/all_gather | solution.py:114
  343.5 5.0 copy-start.5
  371.7 193.4 %reduce-scatter.5.cloned.1.call-start = ((), (), s32[]{:S(2)}) async-start(), calls=%async_computation.9 | async-start | bytes 2949120 | tf_op jit(solution)/shard_map/reduce_scatter | solution.py:150
Sparse Core Ops, SparseCore 0:
  15.1 44.4 all-gather.6
  65.3 55.3 all-gather.10
  123.7 53.1 all-gather.8
  244.4 42.2 reduce-scatter.2
  292.9 44.8 all-gather.12
  343.5 55.3 all-gather.16
  401.9 53.1 all-gather.14
  522.8 42.2 reduce-scatter.4
where the time goes:
time: 576 us; the launch traced here: 575 us
  waiting for transfers between devices  340 us (59%)
  matrix products  70.7 us (12%)
  local copies, waits for them, and re-layouts  63.3 us (11%)
  blocking collectives  36.4 us (6%)
  loops' own time  23 us (4%)
  other arithmetic  22.8 us (4%)
  between operations  16.3 us (3%)
    all_gather x2, waiting for transfers between devices, on_device(): piece_keys = lax.all_gather(keys, 'queue', axis=0, tiled=True)  112 us
    all_gather x2, waiting for transfers between devices, on_device(): piece = lax.all_gather(normed, 'head', axis=0, tiled=True)  89.5 us
    reduce_scatter x2, waiting for transfers between devices, on_device(): lax.psum_scatter(jnp.dot(attn, w_out, preferred_element_type=jnp.float32)...  83.5 us
    dynamic_slice x128, local copies, waits for them, and re-layouts, on_device(): lax.scan(one_block, inner, (piece_keys.reshape(blocks, span, features), p...  61.6 us
    all_gather x2, waiting for transfers between devices, on_device(): piece_values = lax.all_gather(values, 'queue', axis=0, tiled=True)  52.5 us
    psum x2, blocking collectives, on_device(): lax.psum((jnp.sum(q * q, axis=-1), jnp.sum(k * k, axis=-1)), 'head')  36.4 us
    another operation x2, loops' own time, on_device(): lax.scan(one_block, inner, (piece_keys.reshape(blocks, span, features), p...  23 us
    dot_general x32, matrix products, absorb(): jnp.einsum('hqk,khd->hqd', weights.astype(jnp.bfloat16), value_heads, pre...  18.8 us
  transfers between devices with their start and end apart: 9, of which 9 were waited for; matrix products, arithmetic and copies ran while one was open for 4% of the time, Pallas kernels for 0%

commit v1 on v0

v1 whole, which is shorter than its diff:
```python
import functools
import math

import jax
import jax.numpy as jnp
from jax import lax
from jax.experimental import pallas as pl
from jax.experimental.pallas import tpu as pltpu
from jax.sharding import PartitionSpec as P

HD = 128
STEPS = 2
EXTRA = 16
F32, BF16 = jnp.float32, jnp.bfloat16
MIB = 1 << 20


def along_head(array, dx, dy):
    pairs = [(y * 4 + x, ((y + dy) % 2) * 4 + (x + dx) % 4) for y in range(2) for x in range(4)]
    return lax.ppermute(array, "head", pairs)


def along_queue(array, ds, dz, dc):
    pairs = [
        (s * 8 + z * 2 + c, ((s + ds) % 2) * 8 + ((z + dz) % 4) * 2 + (c + dc) % 2)
        for s in range(2)
        for z in range(4)
        for c in range(2)
    ]
    return lax.ppermute(array, "queue", pairs)


def embed(times, width):
    half = width // 2
    freq = jnp.exp(-math.log(10000.0) * jnp.arange(half, dtype=F32) / half)
    angle = times[:, None] * freq[None, :]
    return jnp.concatenate([jnp.cos(angle), jnp.sin(angle)], axis=-1)


def dot(a, b, lhs=1, rhs=0):
    return lax.dot_general(a, b, (((lhs,), (rhs,)), ((), ())), preferred_element_type=F32)


def row_sums(squares):
    ones = jnp.ones((8, squares.shape[1]), BF16)
    high = squares.astype(BF16)
    low = (squares - high.astype(F32)).astype(BF16)
    return dot(ones, high, 1, 1) + dot(ones, low, 1, 1)


def project_kernel(place, *refs):
    blocks, (wq, wk, wv, gq, gk), outs, acc = refs[:8], refs[8:13], refs[13:17], refs[17]
    keep_k, send_k, keep_qv, send_qv = outs
    step, side, core = pl.program_id(0), place[0], place[1]
    rows = jnp.concatenate([block[...] for block in blocks], axis=0)
    n = wq.shape[1]
    parts = [dot(rows, w[...]) for w in (wq, wk, wv)]

    @pl.when(step == 0)
    def _():
        for i, part in enumerate(parts):
            acc[:, i * n : (i + 1) * n] = part

    @pl.when(step > 0)
    def _():
        for i, part in enumerate(parts):
            acc[:, i * n : (i + 1) * n] += part

    @pl.when(step == pl.num_programs(0) - 1)
    def _():
        q, k, v = (acc[:, i * n : (i + 1) * n] for i in range(3))
        count = q.shape[0]
        sums_q, sums_k = row_sums(q * q), row_sums(k * k)
        lines = []
        for sums in (sums_q, sums_k):
            high = sums.astype(BF16).astype(F32)
            for part in (high, sums - high):
                lines += [part[:, :HD], part[:, HD:]]
        line = lax.broadcasted_iota(jnp.int32, (EXTRA, HD), 0)
        extra = jnp.zeros((EXTRA, HD), F32)
        for i, values in enumerate(lines):
            extra = jnp.where(line == i, jnp.concatenate([values, values], axis=0), extra)
        extra = extra.astype(BF16)
        q = (q * gq[...]).astype(BF16)
        k = (k * gk[...]).astype(BF16)
        v = v.astype(BF16)
        for head in range(4):
            own = jnp.where(side == head // 2, 0, 1)
            cut = slice(head * HD, (head + 1) * HD)

            def put(to_k, to_qv):
                to_k[own, :count] = k[:, cut]
                to_k[own, count:] = extra
                to_qv[own, 0] = q[:, cut]
                to_qv[own, 1] = v[:, cut]

            @pl.when(core == head % 2)
            def _():
                put(keep_k, keep_qv)

            @pl.when(core != head % 2)
            def _():
                put(send_k, send_qv)


def project(place, blocks, wq, wk, wv, gq, gk):
    block_rows, depth = blocks[0].shape
    rows, n, tile = 8 * block_rows, wq.shape[1], 1024
    k_shape = jax.ShapeDtypeStruct((2, rows + EXTRA, HD), BF16)
    qv_shape = jax.ShapeDtypeStruct((2, 2, rows, HD), BF16)
    whole = lambda shape: pl.BlockSpec(shape, lambda i, place: (0,) * len(shape))
    return pl.pallas_call(
        project_kernel,
        grid_spec=pltpu.PrefetchScalarGridSpec(
            num_scalar_prefetch=1,
            grid=(depth // tile,),
            in_specs=[pl.BlockSpec((block_rows, tile), lambda i, place: (0, i))] * 8
            + [pl.BlockSpec((tile, n), lambda i, place: (i, 0))] * 3
            + [whole((1, n))] * 2,
            out_specs=[whole(k_shape.shape)] * 2 + [whole(qv_shape.shape)] * 2,
            scratch_shapes=[pltpu.VMEM((rows, 3 * n), F32)],
        ),
        out_shape=[k_shape, k_shape, qv_shape, qv_shape],
        compiler_params=pltpu.CompilerParams(vmem_limit_bytes=40 * MIB),
        cost_estimate=pl.CostEstimate(
            flops=6 * rows * depth * n, bytes_accessed=6 * depth * n, transcendentals=0
        ),
        name="project",
    )(place, *blocks, wq, wk, wv, gq[None, :], gk[None, :])


def attend_kernel(every, slots, lowers, places, sums, q, *refs):
    ks, vs, (o_own, o_sib, o_far), (keys, values, totals) = refs[:4], refs[4:8], refs[8:11], refs[11:]
    count = q.shape[2]
    scale = lax.rsqrt(sums[...] * (1.0 / every) + 1e-6)
    pad = jnp.zeros((HD - 16, HD), F32)
    lines = [
        jnp.concatenate([scale[:, i * HD : (i + 1) * HD], pad], axis=0).T for i in range(4)
    ]
    q_scale = jnp.concatenate(lines[:2], axis=0)
    k_scale = jnp.concatenate(lines[2:], axis=0)
    for at in range(16):
        where = places[at]
        k = ks[at // 4][at % 4, :count].astype(F32)
        keys[where] = (k * k_scale[:, at : at + 1]).astype(BF16)
        values[where] = vs[at // 4][at % 4]
    for span, out in enumerate((o_own.at[:], o_sib.at[:], o_far.at[0], o_far.at[1])):
        queries = q[span // 2, span % 2].astype(F32) * (
            q_scale[:, span : span + 1] * (1.0 / math.sqrt(HD))
        )
        queries = queries.astype(BF16)

        def block(j, carry):
            top, total, acc = carry
            scores = dot(keys[j], queries, 1, 1)
            new_top = jnp.maximum(top, jnp.max(scores, axis=0, keepdims=True))
            weights = jnp.exp(scores - new_top)
            fade = jnp.exp(top - new_top)
            total = total * fade + jnp.sum(weights, axis=0, keepdims=True)
            acc = acc * fade + dot(values[j], weights.astype(BF16), 0, 0)
            return new_top, total, acc

        start = (
            jnp.full((1, count), -1e30, F32),
            jnp.zeros((1, count), F32),
            jnp.zeros((HD, count), F32),
        )
        _, total, acc = lax.fori_loop(lowers[span], slots[span] + 1, block, start)
        out[...] = (acc / total).T.astype(BF16)


def attend(slots, lowers, places, sums, q, ks, vs, every):
    rows = q.shape[2]
    out = jax.ShapeDtypeStruct((rows, HD), BF16)
    vmem = pl.BlockSpec(memory_space=pltpu.VMEM)
    smem = pl.BlockSpec(memory_space=pltpu.SMEM)
    return pl.pallas_call(
        functools.partial(attend_kernel, every),
        in_specs=[smem] * 3 + [vmem] * 10,
        out_specs=[vmem] * 3,
        out_shape=[out, out, jax.ShapeDtypeStruct((2, rows, HD), BF16)],
        scratch_shapes=[
            pltpu.VMEM((16, rows, HD), BF16),
            pltpu.VMEM((16, rows, HD), BF16),
            pltpu.VMEM((8, rows), F32),
        ],
        compiler_params=pltpu.CompilerParams(vmem_limit_bytes=40 * MIB),
        cost_estimate=pl.CostEstimate(
            flops=4 * 32 * rows * rows * HD, bytes_accessed=4 * MIB, transcendentals=32 * rows * rows
        ),
        name="attend",
    )(slots, lowers, places, sums, q, *ks, *vs)


def mix_kernel(place, own, far, near, w, out, acts):
    side, core = place[0], place[1]
    rows = own.shape[0]

    @pl.when(pl.program_id(0) == 0)
    def _():
        for values, s, c in (
            (own[...], side, core),
            (far[0], 1 - side, core),
            (near[0], side, 1 - core),
            (near[1], 1 - side, 1 - core),
        ):
            acts[:, pl.ds(pl.multiple_of((2 * s + c) * HD, HD), HD)] = values

    product = dot(acts[...], w[...]).astype(BF16)
    step = rows // 8
    for i in range(8):
        out[place[2 + i]] = product[i * step : (i + 1) * step]


def mix(place, own, far, near, w):
    rows, depth, width, tile = own.shape[0], w.shape[0], w.shape[1], 1024
    whole = lambda shape: pl.BlockSpec(shape, lambda i, place: (0,) * len(shape))
    return pl.pallas_call(
        mix_kernel,
        grid_spec=pltpu.PrefetchScalarGridSpec(
            num_scalar_prefetch=1,
            grid=(width // tile,),
            in_specs=[whole(own.shape), whole(far.shape), whole(near.shape)]
            + [pl.BlockSpec((depth, tile), lambda i, place: (0, i))],
            out_specs=pl.BlockSpec((8, rows // 8, tile), lambda i, place: (0, 0, i)),
            scratch_shapes=[pltpu.VMEM((rows, depth), BF16)],
        ),
        out_shape=jax.ShapeDtypeStruct((8, rows // 8, width), BF16),
        compiler_params=pltpu.CompilerParams(vmem_limit_bytes=40 * MIB),
        cost_estimate=pl.CostEstimate(
            flops=2 * rows * depth * width, bytes_accessed=2 * depth * width, transcendentals=0
        ),
        name="mix",
    )(place, own, far, near, w)


def gather_blocks(block):
    left, right = along_head(block, 1, 0), along_head(block, -1, 0)
    other = along_head(block, 0, 1)
    across = along_head(block, 2, 0)
    other_left, other_right = along_head(other, 1, 0), along_head(other, -1, 0)
    other_across = along_head(across, 0, 1)
    return [block, right, across, left, other, other_right, other_across, other_left]


def sum_over_head(sums):
    turn = lambda array, by: jnp.concatenate([array[:, :, :, by:], array[:, :, :, :by]], axis=3)
    sums = sums + turn(along_head(sums, 1, 0), 1)
    sums = sums + turn(along_head(sums, 2, 0), 2)
    return sums + along_head(sums, 0, 1)[:, :, ::-1]


def on_device(
    latent, fresh, levels, windows, plan, mod_table, w_query, w_key, w_value, w_out, query_gain, key_gain
):
    queue_count, head_count = lax.axis_size("queue"), lax.axis_size("head")
    slot, head = lax.axis_index("queue"), lax.axis_index("head")
    rows = latent.shape[0]
    span = rows * head_count
    every = w_query.shape[1] * head_count
    side, z, core = slot // 8, (slot // 2) % 4, slot % 2
    places = jnp.stack(
        [
            ((side + s) % 2) * 8 + ((z + dz) % 4) * 2 + (core + c) % 2
            for dz in range(4)
            for s in range(2)
            for c in range(2)
        ]
    )
    blocks_at = [((head // 4 + dy) % 2) * 4 + (head % 4 + dx) % 4 for dy in range(2) for dx in range(4)]
    place = jnp.stack([side, core] + blocks_at)
    lower_all = jnp.maximum(0, jnp.arange(queue_count, dtype=jnp.int32) - windows + 1)
    q_slots = places[:4]
    q_lowers = lower_all[q_slots]

    table_hits = levels[:, None] == jnp.arange(plan.shape[0], dtype=jnp.int32)[None, :]
    t_all = jnp.sum(jnp.where(table_hits, plan[None, :], 0), axis=1).astype(F32)
    t_from = t_all[slot]
    t_to = jnp.where(slot > 0, t_all[jnp.maximum(slot - 1, 0)], 0.0)
    step_size = (t_to - t_from) / 1000.0
    emb = embed(t_from[None], latent.shape[1])[0]
    shift = mod_table[0] + emb
    scale = mod_table[1] + emb
    gate = mod_table[2] + emb
    state = latent
    speeds = []
    new = latent
    for step in range(STEPS):
        with jax.named_scope("norm"):
            x = state.astype(F32)
            mean = jnp.mean(x, axis=-1, keepdims=True)
            var = jnp.mean((x - mean) ** 2, axis=-1, keepdims=True)
            normed = ((x - mean) * lax.rsqrt(var + 1e-06) * (1.0 + scale) + shift).astype(BF16)
        with jax.named_scope("gather"):
            blocks = gather_blocks(normed)
        with jax.named_scope("project"):
            keep_k, send_k, keep_qv, send_qv = project(
                place, blocks, w_query, w_key, w_value, query_gain, key_gain
            )
        with jax.named_scope("swap"):
            core_k = along_queue(send_k, 0, 0, 1)
            core_qv = along_queue(send_qv, 0, 0, 1)
            far_k = along_queue(jnp.stack([keep_k[1], core_k[1]]), 1, 0, 0)
            own_k = jnp.stack([keep_k[0], core_k[0], far_k[0], far_k[1]])
            far_qv = along_queue(jnp.stack([keep_qv[1], core_qv[1]]), 1, 0, 0)
            own_v = jnp.stack([keep_qv[0, 1], core_qv[0, 1], far_qv[0, 1], far_qv[1, 1]])
            own_q = jnp.stack([keep_qv[0, 0], core_qv[0, 0], far_qv[0, 0], far_qv[1, 0]]).reshape(
                2, 2, span, HD
            )
        with jax.named_scope("ring"):
            ks = [own_k] + [along_queue(own_k, 0, -dz, 0) for dz in (1, 2, 3)]
            vs = [own_v] + [along_queue(own_v, 0, -dz, 0) for dz in (1, 2, 3)]
        with jax.named_scope("sums"):
            lines = jnp.concatenate([k[:, span : span + 8] for k in ks], axis=0).astype(F32)
            lines = lines.reshape(16, 2, 2, 2, HD)
            sums = (lines[:, :, 0] + lines[:, :, 1]).reshape(16, 2, 2, 4, HD // 4)
            sums = sum_over_head(sums).reshape(16, 4 * HD)
        with jax.named_scope("attend"):
            o_own, o_sib, o_far = attend(q_slots, q_lowers, places, sums, own_q, ks, vs, every)
        with jax.named_scope("back"):
            far = along_queue(o_far, 1, 0, 0)
            near = along_queue(jnp.stack([o_sib, far[1]]), 0, 0, 1)
        with jax.named_scope("mix"):
            product = mix(place, o_own, far, near, w_out)
        with jax.named_scope("reduce"):
            mixed = jnp.sum(lax.all_to_all(product, "head", 0, 0).astype(F32), axis=0)
        with jax.named_scope("update"):
            speed = (x + gate * mixed).astype(BF16)
            speeds.append(speed)
            new = (x + step_size * speed.astype(F32)).astype(BF16)
            if step < STEPS - 1:
                moved = lax.ppermute(new, "queue", [(i, i - 1) for i in range(1, queue_count)])
                state = jnp.where(slot == queue_count - 1, fresh, moved)
    return (jnp.stack(speeds), new)


def solution(mesh):
    return jax.shard_map(
        on_device,
        mesh=mesh,
        in_specs=(
            P(("queue", "head"), None),
            P("head", None),
            P(),
            P(),
            P(),
            P(),
            P(None, "head"),
            P(None, "head"),
            P(None, "head"),
            P("head", None),
            P("head"),
            P("head"),
        ),
        out_specs=(P(None, ("queue", "head"), None), P(("queue", "head"), None)),
        check_vma=False,
    )
```

time: 576 us -> 337 us (0.59)
  waiting for transfers between devices: 340 us -> 125 us
  starting transfers between devices: 1.8 us -> 91.6 us
  matrix products: 70.7 us -> 0 us
  local copies, waits for them, and re-layouts: 63.3 us -> 18.7 us
  Pallas kernels: 0 us -> 42.4 us
  loops' own time: 23 us -> 0 us
  between operations: 16.3 us -> 2.4 us
  other arithmetic: 22.8 us -> 13.3 us
    all_gather x6 -> x0, waiting for transfers between devices: 255 us -> none  [the longest x2 112 us: on_device(): piece_keys = lax.all_gather(keys, 'queue', axis=0, tiled=True)]
    ppermute x1 -> x45, waiting for transfers between devices: 2.22 us -> 93.3 us  [the longest x20 48.4 us: along_head(): return lax.ppermute(array, 'head', pairs)]
    ppermute x1 -> x45, starting transfers between devices: 1.29 us -> 87.1 us  [the longest x24 52.2 us: along_queue(): return lax.ppermute(array, 'queue', pairs)]
    reduce_scatter x2 -> x0, waiting for transfers between devices: 83.5 us -> none  [on_device(): lax.psum_scatter(jnp.dot(attn, w_out, preferred_element_type=jnp.float32)...]
    dot_general x72 -> x0, matrix products: 70.7 us -> none  [the longest x32 18.8 us: absorb(): jnp.einsum('hqk,khd->hqd', weights.astype(jnp.bfloat16), value_heads, pre...]
    dynamic_slice x129 -> x0, local copies, waits for them, and re-layouts: 62.2 us -> none  [the longest x128 61.6 us: on_device(): lax.scan(one_block, inner, (piece_keys.reshape(blocks, span, features), p...]
    pallas_call x0 -> x6, Pallas kernels: none -> 42.4 us  [the longest x2 17.4 us: attend(): pl.pallas_call(functools.partial(attend_kernel, every), in_specs=[smem] *...]
    all_to_all x0 -> x1, blocking collectives: none -> 37.1 us  [on_device(): mixed = jnp.sum(lax.all_to_all(product, 'head', 0, 0).astype(F32), axis=0)]
  transfers between devices with their start and end apart: 9 -> 46, of which waited for: 9 -> 30; matrix products, arithmetic and copies ran while one was open for 4% -> 1% of each run, Pallas kernels for 0% -> 0%
where the time goes in v1:
time: 337 us; the launch traced here: 331 us
  waiting for transfers between devices  125 us (37%)
  starting transfers between devices  91.6 us (27%)
  Pallas kernels  42.4 us (13%)
  blocking collectives  37.1 us (11%)
  local copies, waits for them, and re-layouts  18.7 us (6%)
  other arithmetic  13.3 us (4%)
    ppermute x24, starting transfers between devices, along_queue(): return lax.ppermute(array, 'queue', pairs)  52.2 us
    ppermute x20, waiting for transfers between devices, along_head(): return lax.ppermute(array, 'head', pairs)  48.4 us
    ppermute x24, waiting for transfers between devices, along_queue(): return lax.ppermute(array, 'queue', pairs)  42.6 us
    all_to_all x1, blocking collectives, on_device(): mixed = jnp.sum(lax.all_to_all(product, 'head', 0, 0).astype(F32), axis=0)  37.1 us
    ppermute x20, starting transfers between devices, along_head(): return lax.ppermute(array, 'head', pairs)  33.6 us
    all_to_all x1, waiting for transfers between devices, on_device(): mixed = jnp.sum(lax.all_to_all(product, 'head', 0, 0).astype(F32), axis=0)  31.9 us
    pallas_call x2, Pallas kernels, attend(): pl.pallas_call(functools.partial(attend_kernel, every), in_specs=[smem] *...  17.4 us
    pallas_call x2, Pallas kernels, project(): pl.pallas_call(project_kernel, grid_spec=pltpu.PrefetchScalarGridSpec(num...  16.9 us
  transfers between devices with their start and end apart: 46, of which 30 were waited for; matrix products, arithmetic and copies ran while one was open for 1% of the time, Pallas kernels for 0%

profile of v1, /device:TPU:0, one launch (start us, length us, event | category | flops | bytes accessed | tf_op | source)
XLA Modules:
  0.0 330.7 jit_solution(986492359987371607)
XLA Ops:
  9.5 3.0 collective-permute-start.1
  23.8 3.9 %collective-permute-done.2.refs_3_ = bf16[32,5120]{1,0:T(8,128)(2,1)S(1)} collective-permute-done((bf16[32,5120]{1,0:T(8,128)(2,1)S(1)}, bf16[32,5120]{1,0:T(8,128)(2,1)S(1)}, u32[]{:S(2)}, u32[]{:S(2)}) %collective-permute-start.2) | collective-permute-done | bytes 327712 | tf_op jit(solution)/shard_map/gather/ppermute | solution.py:20
  28.8 5.4 %collective-permute-done.6.refs_7_ = bf16[32,5120]{1,0:T(8,128)(2,1)S(1)} collective-permute-done((bf16[32,5120]{1,0:T(8,128)(2,1)S(1)}, bf16[32,5120]{1,0:T(8,128)(2,1)S(1)}, u32[]{:S(2)}, u32[]{:S(2)}) %collective-permute-start.6) | collective-permute-done | bytes 327712 | tf_op jit(solution)/shard_map/gather/ppermute | solution.py:20
  40.7 8.5 %project.2 = (bf16[2,272,128]{2,1,0:T(8,128)(2,1)S(1)}, bf16[2,272,128]{2,1,0:T(8,128)(2,1)S(1)}, bf16[2,2,256,128]{3,2,1,0:T(8,128)(2,1)S(1)}, bf16[2,2,256,128]{3,2,1,0:T(8,128)(2,1)S(1)}) custom-call(s32[10]{0:T(128)S(1)} %stack.157.place, bf16[32,5120]{1,0:T(8,128)(2,1)S(1)} %fusion.11.refs_0_, bf16[32,5120]{1,0:T(8,128)(2,1)S(1)} %collective-permute-done.refs_1_, ...), custom_call_target="tpu_custom_call" | custom-call | flops 4026531840 | bytes 15728640 | tf_op jit(solution)/shard_map/project/project/pallas_call | solution.py:112
  53.7 4.3 %collective-permute-done.8 = bf16[2,272,128]{2,1,0:T(8,128)(2,1)S(1)} collective-permute-done((bf16[2,272,128]{2,1,0:T(8,128)(2,1)S(1)}, bf16[2,272,128]{2,1,0:T(8,128)(2,1)S(1)}, u32[]{:S(2)}, u32[]{:S(2)}) %collective-permute-start.8) | collective-permute-done | bytes 139296 | tf_op jit(solution)/shard_map/swap/ppermute | solution.py:30
  60.0 3.6 %collective-permute-start.10 = (bf16[4,272,128]{2,1,0:T(8,128)(2,1)S(1)}, bf16[4,272,128]{2,1,0:T(8,128)(2,1)S(1)}, u32[]{:S(2)}, u32[]{:S(2)}) collective-permute-start(bf16[4,272,128]{2,1,0:T(8,128)(2,1)S(1)} %pad_maximum_fusion.1.refs_0_), channel_id=1, source_target_pairs={{0,32},{8,40},{16,48},{24,56},{32,0},{40,8},{48,16},{56,24},{64,96... | collective-permute-start | bytes 835592 | tf_op jit(solution)/shard_map/ring/ppermute | solution.py:30
  64.6 3.0 collective-permute-start.16
  68.8 6.6 %collective-permute-done.10.refs_2_ = bf16[4,272,128]{2,1,0:T(8,128)(2,1)S(1)} collective-permute-done((bf16[4,272,128]{2,1,0:T(8,128)(2,1)S(1)}, bf16[4,272,128]{2,1,0:T(8,128)(2,1)S(1)}, u32[]{:S(2)}, u32[]{:S(2)}) %collective-permute-start.10) | collective-permute-done | bytes 278560 | tf_op jit(solution)/shard_map/ring/ppermute | solution.py:30
  77.2 4.7 %collective-permute-done.12 = f32[16,2,2,4,32]{4,3,2,1,0:T(4,128)S(1)} collective-permute-done((f32[16,2,2,4,32]{4,3,2,1,0:T(4,128)S(1)}, f32[16,2,2,4,32]{4,3,2,1,0:T(4,128)S(1)}, u32[]{:S(2)}, u32[]{:S(2)}) %collective-permute-start.12) | collective-permute-done | bytes 32800 | tf_op jit(solution)/shard_map/sums/ppermute | solution.py:20
  89.3 4.5 %collective-permute-done.14 = f32[16,2,2,4,32]{4,3,2,1,0:T(4,128)S(1)} collective-permute-done((f32[16,2,2,4,32]{4,3,2,1,0:T(4,128)S(1)}, f32[16,2,2,4,32]{4,3,2,1,0:T(4,128)S(1)}, u32[]{:S(2)}, u32[]{:S(2)}) %collective-permute-start.14) | collective-permute-done | bytes 32800 | tf_op jit(solution)/shard_map/sums/ppermute | solution.py:20
  94.0 3.8 %collective-permute-done.18.refs_6_ = bf16[4,256,128]{2,1,0:T(8,128)(2,1)S(1)} collective-permute-done((bf16[4,256,128]{2,1,0:T(8,128)(2,1)S(1)}, bf16[4,256,128]{2,1,0:T(8,128)(2,1)S(1)}, u32[]{:S(2)}, u32[]{:S(2)}) %collective-permute-start.18) | collective-permute-done | bytes 262176 | tf_op jit(solution)/shard_map/ring/ppermute | solution.py:30
  97.8 8.8 %attend.2 = (bf16[256,128]{1,0:T(8,128)(2,1)S(1)}, bf16[256,128]{1,0:T(8,128)(2,1)S(1)}, bf16[2,256,128]{2,1,0:T(8,128)(2,1)S(1)}) custom-call(s32[4]{0:T(128)S(1)} %pad_add_fusion.slots, s32[4]{0:T(128)S(1)} %gather_fusion, s32[16]{0:T(128)S(1)} %stack.180.places, f32[16,512]{1,0:T(8,128)S(1)} %reshape.247.sums, bf16[2,2,256,128]{3,2,1,0:T(8,128)(2,1)S(1)} %bitcast.88, ...), custom_call_target="tpu_custom_call" | custom-call | flops 1073741824 | bytes 4194304 | tf_op jit(solution)/shard_map/attend/attend/pallas_call | solution.py:177
  106.6 3.0 collective-permute-start.20
  109.6 3.6 %collective-permute-done.20.far = bf16[2,256,128]{2,1,0:T(8,128)(2,1)S(1)} collective-permute-done((bf16[2,256,128]{2,1,0:T(8,128)(2,1)S(1)}, bf16[2,256,128]{2,1,0:T(8,128)(2,1)S(1)}, u32[]{:S(2)}, u32[]{:S(2)}) %collective-permute-start.20) | collective-permute-done | bytes 131104 | tf_op jit(solution)/shard_map/back/ppermute | solution.py:30
  117.1 4.7 %mix.2 = bf16[8,32,5120]{2,1,0:T(8,128)(2,1)} custom-call(s32[10]{0:T(128)S(1)} %stack.157.place, bf16[256,128]{1,0:T(8,128)(2,1)S(1)} %get-tuple-element.20.own, bf16[2,256,128]{2,1,0:T(8,128)(2,1)S(1)} %collective-permute-done.20.far, bf16[2,256,128]{2,1,0:T(8,128)(2,1)S(1)} %collective-permute-done.21.near, bf16[512,5120]{1,0:T(8,128)(2,1)S(1)} %copy-done), custom_call_target="tpu_custom_call" | custom-call | flops 1342177280 | bytes 5242880 | tf_op jit(solution)/shard_map/mix/mix/pallas_call | solution.py:218
  121.8 4.5 %all-to-all-start = ((bf16[8,32,5120]{2,1,0:T(8,128)(2,1)}), bf16[8,32,5120]{2,1,0:T(8,128)(2,1)}, u32[]{:S(2)}, u32[]{:S(2)}) async-start(bf16[8,32,5120]{2,1,0:T(8,128)(2,1)} %mix.2), calls=%async_computation | async-start | bytes 5242880 | tf_op jit(solution)/shard_map/reduce/all_to_all | solution.py:326
  127.6 31.9 %all-to-all-done = bf16[8,32,5120]{2,1,0:T(8,128)(2,1)} async-done(((bf16[8,32,5120]{2,1,0:T(8,128)(2,1)}), bf16[8,32,5120]{2,1,0:T(8,128)(2,1)}, u32[]{:S(2)}, u32[]{:S(2)}) %all-to-all-start) | async-done | bytes 2621472 | tf_op jit(solution)/shard_map/reduce/all_to_all | solution.py:326
  169.5 7.9 %collective-permute-start.25 = (bf16[32,5120]{1,0:T(8,128)(2,1)S(1)}, bf16[32,5120]{1,0:T(8,128)(2,1)S(1)}, u32[]{:S(2)}, u32[]{:S(2)}) collective-permute-start(bf16[32,5120]{1,0:T(8,128)(2,1)S(1)} %fusion.7.refs_0_), channel_id=1, source_target_pairs={{0,1},{1,2},{2,3},{3,0},{4,5},{5,6},{6,7},{7,4},{8,9},{9,10},{10,1... | collective-permute-start | bytes 983048 | tf_op jit(solution)/shard_map/gather/ppermute | solution.py:20
  183.6 7.5 %collective-permute-done.23.refs_1_ = bf16[32,5120]{1,0:T(8,128)(2,1)S(1)} collective-permute-done((bf16[32,5120]{1,0:T(8,128)(2,1)S(1)}, bf16[32,5120]{1,0:T(8,128)(2,1)S(1)}, u32[]{:S(2)}, u32[]{:S(2)}) %collective-permute-start.23) | collective-permute-done | bytes 327712 | tf_op jit(solution)/shard_map/gather/ppermute | solution.py:20
  191.1 7.0 %collective-permute-done.27.refs_5_ = bf16[32,5120]{1,0:T(8,128)(2,1)S(1)} collective-permute-done((bf16[32,5120]{1,0:T(8,128)(2,1)S(1)}, bf16[32,5120]{1,0:T(8,128)(2,1)S(1)}, u32[]{:S(2)}, u32[]{:S(2)}) %collective-permute-start.27) | collective-permute-done | bytes 327712 | tf_op jit(solution)/shard_map/gather/ppermute | solution.py:20
  203.1 8.4 %project.3 = (bf16[2,272,128]{2,1,0:T(8,128)(2,1)S(1)}, bf16[2,272,128]{2,1,0:T(8,128)(2,1)S(1)}, bf16[2,2,256,128]{3,2,1,0:T(8,128)(2,1)S(1)}, bf16[2,2,256,128]{3,2,1,0:T(8,128)(2,1)S(1)}) custom-call(s32[10]{0:T(128)S(1)} %stack.157.place, bf16[32,5120]{1,0:T(8,128)(2,1)S(1)} %fusion.7.refs_0_, bf16[32,5120]{1,0:T(8,128)(2,1)S(1)} %collective-permute-done.23.refs_1_, ...), custom_call_target="tpu_custom_call" | custom-call | flops 4026531840 | bytes 15728640 | tf_op jit(solution)/shard_map/project/project/pallas_call | solution.py:112
  214.4 7.3 %collective-permute-start.31 = (bf16[2,272,128]{2,1,0:T(8,128)(2,1)S(1)}, bf16[2,272,128]{2,1,0:T(8,128)(2,1)S(1)}, u32[]{:S(2)}, u32[]{:S(2)}) collective-permute-start(bf16[2,272,128]{2,1,0:T(8,128)(2,1)S(1)} %pad_maximum_fusion.10), channel_id=1, source_target_pairs={{0,64},{8,72},{16,80},{24,88},{32,96},{40,104},{48,112},{56,120},{... | collective-permute-start | bytes 417800 | tf_op jit(solution)/shard_map/swap/ppermute | solution.py:30
  221.8 3.9 %collective-permute-done.31 = bf16[2,272,128]{2,1,0:T(8,128)(2,1)S(1)} collective-permute-done((bf16[2,272,128]{2,1,0:T(8,128)(2,1)S(1)}, bf16[2,272,128]{2,1,0:T(8,128)(2,1)S(1)}, u32[]{:S(2)}, u32[]{:S(2)}) %collective-permute-start.31) | collective-permute-done | bytes 139296 | tf_op jit(solution)/shard_map/swap/ppermute | solution.py:30
  226.8 8.1 %collective-permute-start.33 = (bf16[4,272,128]{2,1,0:T(8,128)(2,1)S(1)}, bf16[4,272,128]{2,1,0:T(8,128)(2,1)S(1)}, u32[]{:S(2)}, u32[]{:S(2)}) collective-permute-start(bf16[4,272,128]{2,1,0:T(8,128)(2,1)S(1)} %pad_maximum_fusion.2.refs_0_), channel_id=1, source_target_pairs={{0,32},{8,40},{16,48},{24,56},{32,0},{40,8},{48,16},{56,24},{64,96... | collective-permute-start | bytes 835592 | tf_op jit(solution)/shard_map/ring/ppermute | solution.py:30
  240.1 6.8 %collective-permute-done.33.refs_2_ = bf16[4,272,128]{2,1,0:T(8,128)(2,1)S(1)} collective-permute-done((bf16[4,272,128]{2,1,0:T(8,128)(2,1)S(1)}, bf16[4,272,128]{2,1,0:T(8,128)(2,1)S(1)}, u32[]{:S(2)}, u32[]{:S(2)}) %collective-permute-start.33) | collective-permute-done | bytes 278560 | tf_op jit(solution)/shard_map/ring/ppermute | solution.py:30
  247.3 6.1 %collective-permute-done.35 = f32[16,2,2,4,32]{4,3,2,1,0:T(4,128)S(1)} collective-permute-done((f32[16,2,2,4,32]{4,3,2,1,0:T(4,128)S(1)}, f32[16,2,2,4,32]{4,3,2,1,0:T(4,128)S(1)}, u32[]{:S(2)}, u32[]{:S(2)}) %collective-permute-start.35) | collective-permute-done | bytes 32800 | tf_op jit(solution)/shard_map/sums/ppermute | solution.py:20
  261.2 4.4 %collective-permute-done.37 = f32[16,2,2,4,32]{4,3,2,1,0:T(4,128)S(1)} collective-permute-done((f32[16,2,2,4,32]{4,3,2,1,0:T(4,128)S(1)}, f32[16,2,2,4,32]{4,3,2,1,0:T(4,128)S(1)}, u32[]{:S(2)}, u32[]{:S(2)}) %collective-permute-start.37) | collective-permute-done | bytes 32800 | tf_op jit(solution)/shard_map/sums/ppermute | solution.py:20
  265.8 3.2 collective-permute-done.41.refs_6_
  269.0 8.6 %attend.3 = (bf16[256,128]{1,0:T(8,128)(2,1)S(1)}, bf16[256,128]{1,0:T(8,128)(2,1)S(1)}, bf16[2,256,128]{2,1,0:T(8,128)(2,1)S(1)}) custom-call(s32[4]{0:T(128)S(1)} %pad_add_fusion.slots, s32[4]{0:T(128)S(1)} %gather_fusion, s32[16]{0:T(128)S(1)} %stack.180.places, f32[16,512]{1,0:T(8,128)S(1)} %reshape.249.sums, bf16[2,2,256,128]{3,2,1,0:T(8,128)(2,1)S(1)} %bitcast.87, ...), custom_call_target="tpu_custom_call" | custom-call | flops 1073741824 | bytes 4194304 | tf_op jit(solution)/shard_map/attend/attend/pallas_call | solution.py:177
  279.6 4.6 %collective-permute-done.43.far = bf16[2,256,128]{2,1,0:T(8,128)(2,1)S(1)} collective-permute-done((bf16[2,256,128]{2,1,0:T(8,128)(2,1)S(1)}, bf16[2,256,128]{2,1,0:T(8,128)(2,1)S(1)}, u32[]{:S(2)}, u32[]{:S(2)}) %collective-permute-start.43) | collective-permute-done | bytes 131104 | tf_op jit(solution)/shard_map/back/ppermute | solution.py:30
  288.1 3.4 %mix.3 = bf16[8,32,5120]{2,1,0:T(8,128)(2,1)S(1)} custom-call(s32[10]{0:T(128)S(1)} %stack.157.place, bf16[256,128]{1,0:T(8,128)(2,1)S(1)} %get-tuple-element.27.own, bf16[2,256,128]{2,1,0:T(8,128)(2,1)S(1)} %collective-permute-done.43.far, bf16[2,256,128]{2,1,0:T(8,128)(2,1)S(1)} %collective-permute-done.44.near, bf16[512,5120]{1,0:T(8,128)(2,1)S(1)} %copy-done.1), custom_call_target="tpu_custom_call" | custom-call | flops 1342177280 | bytes 5242880 | tf_op jit(solution)/shard_map/mix/mix/pallas_call | solution.py:218
  291.5 37.1 %all_to_all.10 = bf16[8,32,5120]{2,1,0:T(8,128)(2,1)S(1)} all-to-all(bf16[8,32,5120]{2,1,0:T(8,128)(2,1)S(1)} %mix.3), channel_id=1, replica_groups=mesh['queue'=16,'head'=8] {'head'}, dimensions={0} | all-to-all | bytes 5242880 | tf_op jit(solution)/shard_map/reduce/all_to_all | solution.py:326
  (174 shorter events, 96.1 us)
Async XLA Ops:
  7.8 9.4 %collective-permute-start.3 = (bf16[32,5120]{1,0:T(8,128)(2,1)S(1)}, bf16[32,5120]{1,0:T(8,128)(2,1)S(1)}, u32[]{:S(2)}, u32[]{:S(2)}) collective-permute-start(bf16[32,5120]{1,0:T(8,128)(2,1)S(1)} %fusion.11.refs_0_), channel_id=1, source_target_pairs={{0,4},{1,5},{2,6},{3,7},{4,0},{5,1},{6,2},{7,3},{8,12},{9,13},{10,... | collective-permute-start | bytes 983048 | tf_op jit(solution)/shard_map/gather/ppermute | solution.py:20
  9.5 12.2 %collective-permute-start.1 = (bf16[32,5120]{1,0:T(8,128)(2,1)S(1)}, bf16[32,5120]{1,0:T(8,128)(2,1)S(1)}, u32[]{:S(2)}, u32[]{:S(2)}) collective-permute-start(bf16[32,5120]{1,0:T(8,128)(2,1)S(1)} %fusion.11.refs_0_), channel_id=1, source_target_pairs={{0,2},{1,3},{2,0},{3,1},{4,6},{5,7},{6,4},{7,5},{8,10},{9,11},{10,... | collective-permute-start | bytes 983048 | tf_op jit(solution)/shard_map/gather/ppermute | solution.py:20
  12.6 15.2 %collective-permute-start.2 = (bf16[32,5120]{1,0:T(8,128)(2,1)S(1)}, bf16[32,5120]{1,0:T(8,128)(2,1)S(1)}, u32[]{:S(2)}, u32[]{:S(2)}) collective-permute-start(bf16[32,5120]{1,0:T(8,128)(2,1)S(1)} %fusion.11.refs_0_), channel_id=1, source_target_pairs={{0,1},{1,2},{2,3},{3,0},{4,5},{5,6},{6,7},{7,4},{8,9},{9,10},{10,1... | collective-permute-start | bytes 983048 | tf_op jit(solution)/shard_map/gather/ppermute | solution.py:20
  13.1 15.7 %collective-permute-start = (bf16[32,5120]{1,0:T(8,128)(2,1)S(1)}, bf16[32,5120]{1,0:T(8,128)(2,1)S(1)}, u32[]{:S(2)}, u32[]{:S(2)}) collective-permute-start(bf16[32,5120]{1,0:T(8,128)(2,1)S(1)} %fusion.11.refs_0_), channel_id=1, source_target_pairs={{0,3},{1,0},{2,1},{3,2},{4,7},{5,4},{6,5},{7,6},{8,11},{9,8},{10,9... | collective-permute-start | bytes 983048 | tf_op jit(solution)/shard_map/gather/ppermute | solution.py:20
  17.2 17.0 %collective-permute-start.6 = (bf16[32,5120]{1,0:T(8,128)(2,1)S(1)}, bf16[32,5120]{1,0:T(8,128)(2,1)S(1)}, u32[]{:S(2)}, u32[]{:S(2)}) collective-permute-start(bf16[32,5120]{1,0:T(8,128)(2,1)S(1)} %collective-permute-done.3.refs_4_), channel_id=1, source_target_pairs={{0,1},{1,2},{2,3},{3,0},{4,5},{5,6},{6,7},{7,4},{8,9},{9,10},{10,1... | collective-permute-start | bytes 983048 | tf_op jit(solution)/shard_map/gather/ppermute | solution.py:20
  18.9 15.5 %collective-permute-start.4 = (bf16[32,5120]{1,0:T(8,128)(2,1)S(1)}, bf16[32,5120]{1,0:T(8,128)(2,1)S(1)}, u32[]{:S(2)}, u32[]{:S(2)}) collective-permute-start(bf16[32,5120]{1,0:T(8,128)(2,1)S(1)} %collective-permute-done.3.refs_4_), channel_id=1, source_target_pairs={{0,3},{1,0},{2,1},{3,2},{4,7},{5,4},{6,5},{7,6},{8,11},{9,8},{10,9... | collective-permute-start | bytes 983048 | tf_op jit(solution)/shard_map/gather/ppermute | solution.py:20
  21.7 12.7 %collective-permute-start.5 = (bf16[32,5120]{1,0:T(8,128)(2,1)S(1)}, bf16[32,5120]{1,0:T(8,128)(2,1)S(1)}, u32[]{:S(2)}, u32[]{:S(2)}) collective-permute-start(bf16[32,5120]{1,0:T(8,128)(2,1)S(1)} %collective-permute-done.1.refs_2_), channel_id=1, source_target_pairs={{0,4},{1,5},{2,6},{3,7},{4,0},{5,1},{6,2},{7,3},{8,12},{9,13},{10,... | collective-permute-start | bytes 983048 | tf_op jit(solution)/shard_map/gather/ppermute | solution.py:20
  50.7 7.3 %collective-permute-start.8 = (bf16[2,272,128]{2,1,0:T(8,128)(2,1)S(1)}, bf16[2,272,128]{2,1,0:T(8,128)(2,1)S(1)}, u32[]{:S(2)}, u32[]{:S(2)}) collective-permute-start(bf16[2,272,128]{2,1,0:T(8,128)(2,1)S(1)} %pad_maximum_fusion.9), channel_id=1, source_target_pairs={{0,64},{8,72},{16,80},{24,88},{32,96},{40,104},{48,112},{56,120},{... | collective-permute-start | bytes 417800 | tf_op jit(solution)/shard_map/swap/ppermute | solution.py:30
  58.0 10.8 %collective-permute-start.11 = (bf16[4,272,128]{2,1,0:T(8,128)(2,1)S(1)}, bf16[4,272,128]{2,1,0:T(8,128)(2,1)S(1)}, u32[]{:S(2)}, u32[]{:S(2)}) collective-permute-start(bf16[4,272,128]{2,1,0:T(8,128)(2,1)S(1)} %pad_maximum_fusion.1.refs_0_), channel_id=1, source_target_pairs={{0,16},{8,24},{16,32},{24,40},{32,48},{40,56},{48,0},{56,8},{64,80... | collective-permute-start | bytes 835592 | tf_op jit(solution)/shard_map/ring/ppermute | solution.py:30
  60.0 15.4 %collective-permute-start.10 = (bf16[4,272,128]{2,1,0:T(8,128)(2,1)S(1)}, bf16[4,272,128]{2,1,0:T(8,128)(2,1)S(1)}, u32[]{:S(2)}, u32[]{:S(2)}) collective-permute-start(bf16[4,272,128]{2,1,0:T(8,128)(2,1)S(1)} %pad_maximum_fusion.1.refs_0_), channel_id=1, source_target_pairs={{0,32},{8,40},{16,48},{24,56},{32,0},{40,8},{48,16},{56,24},{64,96... | collective-permute-start | bytes 835592 | tf_op jit(solution)/shard_map/ring/ppermute | solution.py:30
  63.6 11.8 %collective-permute-start.9 = (bf16[4,272,128]{2,1,0:T(8,128)(2,1)S(1)}, bf16[4,272,128]{2,1,0:T(8,128)(2,1)S(1)}, u32[]{:S(2)}, u32[]{:S(2)}) collective-permute-start(bf16[4,272,128]{2,1,0:T(8,128)(2,1)S(1)} %pad_maximum_fusion.1.refs_0_), channel_id=1, source_target_pairs={{0,48},{8,56},{16,0},{24,8},{32,16},{40,24},{48,32},{56,40},{64,11... | collective-permute-start | bytes 835592 | tf_op jit(solution)/shard_map/ring/ppermute | solution.py:30
  64.6 12.5 %collective-permute-start.16 = (bf16[2,2,256,128]{3,2,1,0:T(8,128)(2,1)S(1)}, bf16[2,2,256,128]{3,2,1,0:T(8,128)(2,1)S(1)}, u32[]{:S(2)}, u32[]{:S(2)}) collective-permute-start(bf16[2,2,256,128]{3,2,1,0:T(8,128)(2,1)S(1)} %pad_maximum_fusion.3), channel_id=1, source_target_pairs={{0,64},{8,72},{16,80},{24,88},{32,96},{40,104},{48,112},{56,120},{... | collective-permute-start | bytes 786440 | tf_op jit(solution)/shard_map/swap/ppermute | solution.py:30
  83.0 11.0 %collective-permute-start.19 = (bf16[4,256,128]{2,1,0:T(8,128)(2,1)S(1)}, bf16[4,256,128]{2,1,0:T(8,128)(2,1)S(1)}, u32[]{:S(2)}, u32[]{:S(2)}) collective-permute-start(bf16[4,256,128]{2,1,0:T(8,128)(2,1)S(1)} %pad_maximum_fusion.5.refs_4_), channel_id=1, source_target_pairs={{0,16},{8,24},{16,32},{24,40},{32,48},{40,56},{48,0},{56,8},{64,80... | collective-permute-start | bytes 786440 | tf_op jit(solution)/shard_map/ring/ppermute | solution.py:30
  84.3 13.5 %collective-permute-start.18 = (bf16[4,256,128]{2,1,0:T(8,128)(2,1)S(1)}, bf16[4,256,128]{2,1,0:T(8,128)(2,1)S(1)}, u32[]{:S(2)}, u32[]{:S(2)}) collective-permute-start(bf16[4,256,128]{2,1,0:T(8,128)(2,1)S(1)} %pad_maximum_fusion.5.refs_4_), channel_id=1, source_target_pairs={{0,32},{8,40},{16,48},{24,56},{32,0},{40,8},{48,16},{56,24},{64,96... | collective-permute-start | bytes 786440 | tf_op jit(solution)/shard_map/ring/ppermute | solution.py:30
  87.1 10.7 %collective-permute-start.17 = (bf16[4,256,128]{2,1,0:T(8,128)(2,1)S(1)}, bf16[4,256,128]{2,1,0:T(8,128)(2,1)S(1)}, u32[]{:S(2)}, u32[]{:S(2)}) collective-permute-start(bf16[4,256,128]{2,1,0:T(8,128)(2,1)S(1)} %pad_maximum_fusion.5.refs_4_), channel_id=1, source_target_pairs={{0,48},{8,56},{16,0},{24,8},{32,16},{40,24},{48,32},{56,40},{64,11... | collective-permute-start | bytes 786440 | tf_op jit(solution)/shard_map/ring/ppermute | solution.py:30
  121.8 37.7 %all-to-all-start = ((bf16[8,32,5120]{2,1,0:T(8,128)(2,1)}), bf16[8,32,5120]{2,1,0:T(8,128)(2,1)}, u32[]{:S(2)}, u32[]{:S(2)}) async-start(bf16[8,32,5120]{2,1,0:T(8,128)(2,1)} %mix.2), calls=%async_computation | async-start | bytes 5242880 | tf_op jit(solution)/shard_map/reduce/all_to_all | solution.py:326
  166.1 11.3 %collective-permute-start.26 = (bf16[32,5120]{1,0:T(8,128)(2,1)S(1)}, bf16[32,5120]{1,0:T(8,128)(2,1)S(1)}, u32[]{:S(2)}, u32[]{:S(2)}) collective-permute-start(bf16[32,5120]{1,0:T(8,128)(2,1)S(1)} %fusion.7.refs_0_), channel_id=1, source_target_pairs={{0,4},{1,5},{2,6},{3,7},{4,0},{5,1},{6,2},{7,3},{8,12},{9,13},{10,... | collective-permute-start | bytes 983048 | tf_op jit(solution)/shard_map/gather/ppermute | solution.py:20
  166.7 15.4 %collective-permute-start.24 = (bf16[32,5120]{1,0:T(8,128)(2,1)S(1)}, bf16[32,5120]{1,0:T(8,128)(2,1)S(1)}, u32[]{:S(2)}, u32[]{:S(2)}) collective-permute-start(bf16[32,5120]{1,0:T(8,128)(2,1)S(1)} %fusion.7.refs_0_), channel_id=1, source_target_pairs={{0,2},{1,3},{2,0},{3,1},{4,6},{5,7},{6,4},{7,5},{8,10},{9,11},{10,... | collective-permute-start | bytes 983048 | tf_op jit(solution)/shard_map/gather/ppermute | solution.py:20
  169.5 14.1 %collective-permute-start.25 = (bf16[32,5120]{1,0:T(8,128)(2,1)S(1)}, bf16[32,5120]{1,0:T(8,128)(2,1)S(1)}, u32[]{:S(2)}, u32[]{:S(2)}) collective-permute-start(bf16[32,5120]{1,0:T(8,128)(2,1)S(1)} %fusion.7.refs_0_), channel_id=1, source_target_pairs={{0,1},{1,2},{2,3},{3,0},{4,5},{5,6},{6,7},{7,4},{8,9},{9,10},{10,1... | collective-permute-start | bytes 983048 | tf_op jit(solution)/shard_map/gather/ppermute | solution.py:20
  177.4 13.7 %collective-permute-start.23 = (bf16[32,5120]{1,0:T(8,128)(2,1)S(1)}, bf16[32,5120]{1,0:T(8,128)(2,1)S(1)}, u32[]{:S(2)}, u32[]{:S(2)}) collective-permute-start(bf16[32,5120]{1,0:T(8,128)(2,1)S(1)} %fusion.7.refs_0_), channel_id=1, source_target_pairs={{0,3},{1,0},{2,1},{3,2},{4,7},{5,4},{6,5},{7,6},{8,11},{9,8},{10,9... | collective-permute-start | bytes 983048 | tf_op jit(solution)/shard_map/gather/ppermute | solution.py:20
  177.4 13.7 %collective-permute-start.29 = (bf16[32,5120]{1,0:T(8,128)(2,1)S(1)}, bf16[32,5120]{1,0:T(8,128)(2,1)S(1)}, u32[]{:S(2)}, u32[]{:S(2)}) collective-permute-start(bf16[32,5120]{1,0:T(8,128)(2,1)S(1)} %collective-permute-done.26.refs_4_), channel_id=1, source_target_pairs={{0,1},{1,2},{2,3},{3,0},{4,5},{5,6},{6,7},{7,4},{8,9},{9,10},{10,1... | collective-permute-start | bytes 983048 | tf_op jit(solution)/shard_map/gather/ppermute | solution.py:20
  179.4 18.7 %collective-permute-start.27 = (bf16[32,5120]{1,0:T(8,128)(2,1)S(1)}, bf16[32,5120]{1,0:T(8,128)(2,1)S(1)}, u32[]{:S(2)}, u32[]{:S(2)}) collective-permute-start(bf16[32,5120]{1,0:T(8,128)(2,1)S(1)} %collective-permute-done.26.refs_4_), channel_id=1, source_target_pairs={{0,3},{1,0},{2,1},{3,2},{4,7},{5,4},{6,5},{7,6},{8,11},{9,8},{10,9... | collective-permute-start | bytes 983048 | tf_op jit(solution)/shard_map/gather/ppermute | solution.py:20
  182.1 16.0 %collective-permute-start.28 = (bf16[32,5120]{1,0:T(8,128)(2,1)S(1)}, bf16[32,5120]{1,0:T(8,128)(2,1)S(1)}, u32[]{:S(2)}, u32[]{:S(2)}) collective-permute-start(bf16[32,5120]{1,0:T(8,128)(2,1)S(1)} %collective-permute-done.24.refs_2_), channel_id=1, source_target_pairs={{0,4},{1,5},{2,6},{3,7},{4,0},{5,1},{6,2},{7,3},{8,12},{9,13},{10,... | collective-permute-start | bytes 983048 | tf_op jit(solution)/shard_map/gather/ppermute | solution.py:20
  213.4 8.4 %collective-permute-start.38 = (bf16[2,2,256,128]{3,2,1,0:T(8,128)(2,1)S(1)}, bf16[2,2,256,128]{3,2,1,0:T(8,128)(2,1)S(1)}, u32[]{:S(2)}, u32[]{:S(2)}) collective-permute-start(bf16[2,2,256,128]{3,2,1,0:T(8,128)(2,1)S(1)} %get-tuple-element.26), channel_id=1, source_target_pairs={{0,8},{8,0},{16,24},{24,16},{32,40},{40,32},{48,56},{56,48},{64,72... | collective-permute-start | bytes 786440 | tf_op jit(solution)/shard_map/swap/ppermute | solution.py:30
  214.4 11.3 %collective-permute-start.31 = (bf16[2,272,128]{2,1,0:T(8,128)(2,1)S(1)}, bf16[2,272,128]{2,1,0:T(8,128)(2,1)S(1)}, u32[]{:S(2)}, u32[]{:S(2)}) collective-permute-start(bf16[2,272,128]{2,1,0:T(8,128)(2,1)S(1)} %pad_maximum_fusion.10), channel_id=1, source_target_pairs={{0,64},{8,72},{16,80},{24,88},{32,96},{40,104},{48,112},{56,120},{... | collective-permute-start | bytes 417800 | tf_op jit(solution)/shard_map/swap/ppermute | solution.py:30
  225.8 14.4 %collective-permute-start.34 = (bf16[4,272,128]{2,1,0:T(8,128)(2,1)S(1)}, bf16[4,272,128]{2,1,0:T(8,128)(2,1)S(1)}, u32[]{:S(2)}, u32[]{:S(2)}) collective-permute-start(bf16[4,272,128]{2,1,0:T(8,128)(2,1)S(1)} %pad_maximum_fusion.2.refs_0_), channel_id=1, source_target_pairs={{0,16},{8,24},{16,32},{24,40},{32,48},{40,56},{48,0},{56,8},{64,80... | collective-permute-start | bytes 835592 | tf_op jit(solution)/shard_map/ring/ppermute | solution.py:30
  226.8 20.1 %collective-permute-start.33 = (bf16[4,272,128]{2,1,0:T(8,128)(2,1)S(1)}, bf16[4,272,128]{2,1,0:T(8,128)(2,1)S(1)}, u32[]{:S(2)}, u32[]{:S(2)}) collective-permute-start(bf16[4,272,128]{2,1,0:T(8,128)(2,1)S(1)} %pad_maximum_fusion.2.refs_0_), channel_id=1, source_target_pairs={{0,32},{8,40},{16,48},{24,56},{32,0},{40,8},{48,16},{56,24},{64,96... | collective-permute-start | bytes 835592 | tf_op jit(solution)/shard_map/ring/ppermute | solution.py:30
  234.9 12.1 %collective-permute-start.32 = (bf16[4,272,128]{2,1,0:T(8,128)(2,1)S(1)}, bf16[4,272,128]{2,1,0:T(8,128)(2,1)S(1)}, u32[]{:S(2)}, u32[]{:S(2)}) collective-permute-start(bf16[4,272,128]{2,1,0:T(8,128)(2,1)S(1)} %pad_maximum_fusion.2.refs_0_), channel_id=1, source_target_pairs={{0,48},{8,56},{16,0},{24,8},{32,16},{40,24},{48,32},{56,40},{64,11... | collective-permute-start | bytes 835592 | tf_op jit(solution)/shard_map/ring/ppermute | solution.py:30
  236.9 10.4 %collective-permute-start.39 = (bf16[2,2,256,128]{3,2,1,0:T(8,128)(2,1)S(1)}, bf16[2,2,256,128]{3,2,1,0:T(8,128)(2,1)S(1)}, u32[]{:S(2)}, u32[]{:S(2)}) collective-permute-start(bf16[2,2,256,128]{3,2,1,0:T(8,128)(2,1)S(1)} %pad_maximum_fusion.6), channel_id=1, source_target_pairs={{0,64},{8,72},{16,80},{24,88},{32,96},{40,104},{48,112},{56,120},{... | collective-permute-start | bytes 786440 | tf_op jit(solution)/shard_map/swap/ppermute | solution.py:30
  254.2 11.6 %collective-permute-start.42 = (bf16[4,256,128]{2,1,0:T(8,128)(2,1)S(1)}, bf16[4,256,128]{2,1,0:T(8,128)(2,1)S(1)}, u32[]{:S(2)}, u32[]{:S(2)}) collective-permute-start(bf16[4,256,128]{2,1,0:T(8,128)(2,1)S(1)} %pad_maximum_fusion.8.refs_4_), channel_id=1, source_target_pairs={{0,16},{8,24},{16,32},{24,40},{32,48},{40,56},{48,0},{56,8},{64,80... | collective-permute-start | bytes 786440 | tf_op jit(solution)/shard_map/ring/ppermute | solution.py:30
  255.5 13.5 %collective-permute-start.41 = (bf16[4,256,128]{2,1,0:T(8,128)(2,1)S(1)}, bf16[4,256,128]{2,1,0:T(8,128)(2,1)S(1)}, u32[]{:S(2)}, u32[]{:S(2)}) collective-permute-start(bf16[4,256,128]{2,1,0:T(8,128)(2,1)S(1)} %pad_maximum_fusion.8.refs_4_), channel_id=1, source_target_pairs={{0,32},{8,40},{16,48},{24,56},{32,0},{40,8},{48,16},{56,24},{64,96... | collective-permute-start | bytes 786440 | tf_op jit(solution)/shard_map/ring/ppermute | solution.py:30
  258.3 10.7 %collective-permute-start.40 = (bf16[4,256,128]{2,1,0:T(8,128)(2,1)S(1)}, bf16[4,256,128]{2,1,0:T(8,128)(2,1)S(1)}, u32[]{:S(2)}, u32[]{:S(2)}) collective-permute-start(bf16[4,256,128]{2,1,0:T(8,128)(2,1)S(1)} %pad_maximum_fusion.8.refs_4_), channel_id=1, source_target_pairs={{0,48},{8,56},{16,0},{24,8},{32,16},{40,24},{48,32},{56,40},{64,11... | collective-permute-start | bytes 786440 | tf_op jit(solution)/shard_map/ring/ppermute | solution.py:30
  (26 other events, 316.6 us)
